TPU v7x, 32 devices: a whole 2x2x4 slice. The times are simulated.
32 devices in a mesh: blk: 8 (over y, x, core), grp: 4 (over z).
Axes of the slice: x: 2, y: 2, z: 4, core: 2. Of those that a mesh axis runs over, the one named last changes fastest.
Arguments:
- sky_map: bfloat16 [256, 262144], P(None, ('blk', 'grp')), may hold values from -128 to 128
- fg_templates: bfloat16 [256, 16], replicated, may hold values from -0.375 to 0.375
- cycle_len: int32 [128], P(('blk', 'grp')), may hold values from 512 to 2048, as said below
- beam_profile: float32 [8, 1024], replicated, may hold values from 0.2 to 2
- beam_index: int32 [256], P('blk'), may hold values from 0 to 7
Outputs:
- filtered: float32 [1024, 256, 2, 1024], P(None, 'blk', None, 'grp')
Inputs may be any that keep to these rules, and one draw needn't show every extreme that they name: `cycle_len`: some cycle has exactly 2048 pixels.
All inputs are finite; a program needn't handle non-finite values.
Results may differ from a plain program's by a relative error of at most 0.0064.
Values may be sent and summed in bfloat16 or wider, within the bound.
A program may use at most 192 MiB of HBM per device.

v0:
```python
import jax
import jax.numpy as jnp
from jax import lax
from jax.sharding import PartitionSpec as P

RPIX = 2048
L = 1024
M_DEV = 256


def cycle_table(length, m_width):
    slots = jnp.arange(RPIX, dtype=jnp.int32)
    orders = jnp.arange(m_width, dtype=jnp.int32)
    phase = orders[None, :] * (2 * slots[:, None] + 1) % (2 * length)
    angle = jnp.pi * phase.astype(jnp.float32) / length.astype(jnp.float32)
    weight = jnp.where(slots < length, 1.0, 0.0).astype(jnp.float32) * lax.rsqrt(
        length.astype(jnp.float32)
    )
    table = jnp.concatenate([jnp.cos(angle), -jnp.sin(angle)], axis=1) * weight[:, None]
    return table.astype(jnp.bfloat16)


def theta_table(cycle_ids, n_cycle):
    degrees = jnp.arange(L, dtype=jnp.int32)
    odd = 2 * cycle_ids + 1
    phase = degrees[:, None] * odd[None, :] % (4 * n_cycle)
    angle = jnp.pi * phase.astype(jnp.float32) / (2.0 * n_cycle)
    weight = jnp.sin(jnp.pi * odd.astype(jnp.float32) / (2.0 * n_cycle)) * (
        2.0 / jnp.sqrt(jnp.float32(n_cycle))
    )
    return (jnp.cos(angle) * weight[None, :]).astype(jnp.bfloat16)


def body(sky_map, fg_templates, cycle_len, beam_profile, beam_index):
    n_blk = lax.axis_size("blk")
    n_grp = lax.axis_size("grp")
    cycle_dev = cycle_len.shape[0]
    n_chan = sky_map.shape[0]
    chan_dev = n_chan // n_blk
    m_width = M_DEV * n_grp
    n_cycle = cycle_dev * n_blk * n_grp
    slots = jnp.arange(RPIX, dtype=jnp.int32)
    valid = (slots[None, :] < cycle_len[:, None]).reshape(-1)
    masked = jnp.where(valid[None, :], sky_map, jnp.zeros((), jnp.bfloat16))
    mode_amps = jnp.dot(fg_templates.T, masked, preferred_element_type=jnp.float32).astype(
        jnp.bfloat16
    )
    gram_part = jnp.dot(mode_amps, mode_amps.T, preferred_element_type=jnp.float32)
    cross_part = lax.dot_general(
        mode_amps, masked, (((1,), (1,)), ((), ())), preferred_element_type=jnp.float32
    )
    amps_wide = mode_amps.astype(jnp.float32)
    gram_sum = lax.psum(gram_part, ("blk", "grp"))
    lower = jnp.linalg.cholesky(gram_sum)
    basis = jax.scipy.linalg.solve_triangular(lower, amps_wide, lower=True)
    proj_part = jax.scipy.linalg.solve_triangular(lower, cross_part, lower=True)
    projected = lax.psum(proj_part, ("blk", "grp"))
    correction = jnp.dot(projected.T, basis, precision=lax.Precision.HIGHEST)
    cleaned = (masked.astype(jnp.float32) - correction).astype(jnp.bfloat16)
    pieces = []
    for local in range(cycle_dev):
        block = cleaned[:, local * RPIX : (local + 1) * RPIX]
        table = cycle_table(cycle_len[local], m_width)
        pieces.append(
            jnp.dot(block, table, preferred_element_type=jnp.float32).astype(jnp.bfloat16)
        )
    fourier = jnp.stack(pieces, 0).reshape(cycle_dev, n_chan, 2, m_width)
    position = jnp.arange(n_cycle, dtype=jnp.int32)
    moved = lax.all_to_all(
        lax.all_to_all(fourier, "blk", split_axis=1, concat_axis=0, tiled=True),
        "grp",
        split_axis=3,
        concat_axis=0,
        tiled=True,
    )
    group_id = position // (n_blk * cycle_dev)
    block_id = position // cycle_dev % n_blk
    cycle_ids = (block_id * n_grp + group_id) * cycle_dev + position % cycle_dev
    moved = moved.reshape(n_cycle, chan_dev * 2 * M_DEV)
    theta_tab = theta_table(cycle_ids, n_cycle)
    harmonic = jnp.dot(theta_tab, moved, preferred_element_type=jnp.float32).reshape(
        L, chan_dev, 2, M_DEV
    )
    onehot = (
        beam_index[:, None] == jnp.arange(beam_profile.shape[0], dtype=jnp.int32)[None, :]
    ).astype(jnp.float32)
    profiles = jnp.dot(onehot, beam_profile, precision=lax.Precision.HIGHEST)
    shaped = harmonic * profiles.T[:, :, None, None]
    orders = lax.axis_index("grp") * M_DEV + jnp.arange(M_DEV, dtype=jnp.int32)
    mweight = 0.25 + orders.astype(jnp.float32) / m_width
    weighted = shaped * mweight[None, None, None, :]
    power_part = jnp.sum(weighted * weighted, axis=(0, 2, 3))
    power = lax.psum(power_part, "grp")
    return weighted * lax.rsqrt(power / (2.0 * L * m_width) + 1e-06)[None, :, None, None]


def solution(mesh):
    return jax.shard_map(
        body,
        mesh=mesh,
        in_specs=(P(None, ("blk", "grp")), P(), P(("blk", "grp")), P(), P("blk")),
        out_specs=P(None, "blk", None, "grp"),
        check_vma=False,
    )
```

profile of v0, /device:TPU:0, one launch (start us, length us, event | category | flops | bytes accessed | tf_op | source)
XLA Modules:
  0.0 1085.4 jit_solution(8476107973285526449)
XLA Ops:
  0.0 1.5 fusion.112
  7.3 2.9 convolution_convert_fusion
  10.4 3.4 fusion.50
  16.6 42.1 %psum.21 = f32[16,16]{0,1:T(8,128)S(1)} all-reduce(f32[16,16]{0,1:T(8,128)S(1)} %fusion.113), channel_id=1, replica_groups=mesh['blk'=8,'grp'=4] {'blk','grp'}, use_global_device_ids=true, to_apply=%region_0.1 | all-reduce | flops 256 | bytes 2048 | tf_op jit(solution)/shard_map/psum | solution.py:53
  58.8 1.5 cholesky.16
  61.6 1.2 custom-call.10
  63.4 40.2 %psum.22 = f32[16,256]{1,0:T(8,128)S(1)} all-reduce(f32[16,256]{1,0:T(8,128)S(1)} %fusion.91), channel_id=1, replica_groups=mesh['blk'=8,'grp'=4] {'blk','grp'}, use_global_device_ids=true, to_apply=%region_3.4 | all-reduce | flops 4096 | bytes 32768 | tf_op jit(solution)/shard_map/psum | solution.py:57
  103.6 8.8 fusion.5
  112.5 451.2 %fusion.49 = (f32[2048,1024]{1,0:T(8,128)S(1)}, f32[2048,1024]{1,0:T(8,128)}, f32[2048,1024]{1,0:T(8,128)}, f32[2048,1024]{1,0:T(8,128)}, f32[2048,1024]{1,0:T(8...) fusion(f32[]{:T(128)S(6)} %convert_element_type.91, pred[]{:T(512)S(6)} %lt.110, ...), kind=kLoop, calls=%fused_computation.63 | loop fusion | flops 94371840 | bytes 67117088 | tf_op jit(solution)/shard_map/cos | solution.py:19
  563.6 6.3 fusion.51
  570.8 8.5 fusion.54
  580.1 9.5 fusion.60
  589.6 1.8 stack.18
  591.5 9.5 fusion.57
  601.0 2.6 stack.17
  603.6 7.6 pad_maximum_fusion
  611.2 53.2 %all_to_all.33 = bf16[4,256,2,1024]{3,2,0,1:T(2,128)(2,1)S(1)} all-to-all(bf16[4,256,2,1024]{3,2,0,1:T(2,128)(2,1)S(1)} %pad_maximum_fusion), channel_id=1, replica_groups=mesh['blk'=8,'grp'=4] {'blk'}, dimensions={1} | all-to-all | bytes 8388608 | tf_op jit(solution)/shard_map/all_to_all | solution.py:70
  664.5 2.3 copy.30
  666.8 2.4 copy.31
  669.2 35.1 %copy.32 = bf16[32,32,2,1024]{1,2,0,3:T(2,128)(2,1)} copy(bf16[32,32,2,1024]{3,1,2,0:T(8,128)(2,1)} %bitcast.53) | data formatting | bytes 8388608 | tf_op jit(solution)/shard_map/all_to_all | solution.py:70
  704.3 19.2 %reshape.137 = bf16[4,2,262144]{2,1,0:T(2,128)(2,1)} reshape(bf16[1024,32,2,32]{3,2,1,0:T(2,128)(2,1)} %bitcast.51) | data formatting | bytes 8388608
  723.5 5.2 all-to-all-start.1
  729.0 92.5 %all-to-all-done.1 = bf16[4,2,262144]{2,1,0:T(2,128)(2,1)} async-done(((bf16[4,2,262144]{2,1,0:T(2,128)(2,1)}), bf16[4,2,262144]{2,1,0:T(2,128)(2,1)}, u32[]{:S(2)}, u32[]{:S(2)}) %all-to-all-start.1) | async-done | bytes 4194336 | tf_op jit(solution)/shard_map/all_to_all | solution.py:69
  821.5 12.1 %reshape.138 = bf16[1024,32,2,32]{3,2,1,0:T(2,128)(2,1)} reshape(bf16[4,2,262144]{2,1,0:T(2,128)(2,1)} %all-to-all-done.1) | data formatting | bytes 8388608
  833.6 40.9 %copy.39 = bf16[32,32,2,4,256]{4,3,1,2,0:T(4,128)(2,1)} copy(bf16[32,32,2,4,256]{1,2,0,4,3:T(2,128)(2,1)} %bitcast.52) | data formatting | bytes 8388608 | tf_op jit(solution)/shard_map/all_to_all | solution.py:69
  874.4 8.6 copy.34
  883.0 7.8 reshape.135
  890.8 6.4 copy.35
  897.2 25.8 %multiply_reduce_fusion = (f32[32]{0:T(128)S(1)}, f32[1024,32,2,256]{3,0,2,1:T(8,128)}) fusion(f32[256]{0:T(256)S(1)} %multiply_add_fusion.1, f32[1024,32]{0,1:T(8,128)S(1)} %convolution_bitcast_fusion, bf16[32,2,256,128]{3,2,1,0:T(8,128)(2,1)} %bitcast.57, f32[128]{0:T(128)S(1)} %sine_multiply_fusion, s32[128]{0:T(128)S(1)} %fusion.97), kind=kOutput, calls=%fused_computation | convolution fusion | flops 4364173312 | bytes 71436416 | tf_op jit(solution)/shard_map/dot_general | solution.py:81
  922.9 9.8 psum.23
  932.7 44.6 %fusion = f32[1024,32,2,256]{3,0,2,1:T(8,128)} fusion(f32[1024,32,2,256]{3,0,2,1:T(8,128)} %get-tuple-element.18, f32[32]{0:T(128)S(1)} %add_rsqrt_fusion, f32[256]{0:T(256)S(1)} %multiply_add_fusion.1, f32[1024,32]{0,1:T(8,128)S(1)} %convolution_bitcast_fusion), kind=kLoop, calls=%fused_computation.2 | loop fusion | flops 50331648 | bytes 134349952 | tf_op jit(solution)/shard_map/mul | solution.py:94
  977.3 107.8 %copy.36 = f32[1024,32,2,256]{3,2,1,0:T(2,128)} copy(f32[1024,32,2,256]{3,0,2,1:T(8,128)} %fusion) | data formatting | bytes 134217728 | tf_op jit(solution)/shard_map/mul | solution.py:94
  (30 shorter events, 7.5 us)
Async XLA Ops:
  0.0 728.8 %copy-start = (f32[8,1024]{1,0:T(8,128)S(1)}, f32[8,1024]{1,0:T(8,128)}, u32[]{:S(2)}) copy-start(f32[8,1024]{1,0:T(8,128)} %param.8) | copy-start | bytes 98308
  112.5 451.2 %copy-start.2 = (bf16[256,8192]{1,0:T(8,128)(2,1)}, bf16[256,8192]{1,0:T(8,128)(2,1)S(1)}, u32[]{:S(2)}) copy-start(bf16[256,8192]{1,0:T(8,128)(2,1)S(1)} %fusion.5) | copy-start | bytes 12582916
  723.5 5.3 copy-start.3
  723.5 98.0 %all-to-all-start.1 = ((bf16[4,2,262144]{2,1,0:T(2,128)(2,1)}), bf16[4,2,262144]{2,1,0:T(2,128)(2,1)}, u32[]{:S(2)}, u32[]{:S(2)}) async-start(bf16[4,2,262144]{2,1,0:T(2,128)(2,1)} %reshape.137), calls=%async_computation.1 | async-start | bytes 8388608 | tf_op jit(solution)/shard_map/all_to_all | solution.py:69
  977.3 107.9 %copy-start.1 = (f32[8,1024]{1,0:T(8,128)S(1)}, f32[8,1024]{1,0:T(8,128)}, u32[]{:S(2)}) copy-start(f32[8,1024]{1,0:T(8,128)} %param.8) | copy-start | bytes 98308
where the time goes:
time: 1090 us
  other arithmetic  511 us (47%)
  local copies, waits for them, and re-layouts  250 us (23%)
  blocking collectives  145 us (13%)
  waiting for transfers between devices  92.5 us (8%)
  matrix products  75.8 us (7%)
    cos x1, other arithmetic, cycle_table(): jnp.cos(angle)  451 us
    mul x1, local copies, waits for them, and re-layouts, body(): weighted * lax.rsqrt(power / (2.0 * L * m_width) + 1e-06)[None, :, None,...  108 us
    all_to_all x1, waiting for transfers between devices, body(): lax.all_to_all(lax.all_to_all(fourier, 'blk', split_axis=1, concat_axis=0...  92.5 us
    all_to_all x1, blocking collectives, body(): lax.all_to_all(fourier, 'blk', split_axis=1, concat_axis=0, tiled=True)  53.2 us
    all_to_all x2, local copies, waits for them, and re-layouts, body(): lax.all_to_all(lax.all_to_all(fourier, 'blk', split_axis=1, concat_axis=0...  49.4 us
    mul x1, other arithmetic, body(): weighted * lax.rsqrt(power / (2.0 * L * m_width) + 1e-06)[None, :, None,...  44.6 us
    psum x1, blocking collectives, body(): gram_sum = lax.psum(gram_part, ('blk', 'grp'))  42.1 us
    psum x1, blocking collectives, body(): projected = lax.psum(proj_part, ('blk', 'grp'))  40.2 us
  transfers between devices with their start and end apart: 1, of which 1 were waited for; matrix products, arithmetic and copies ran while one was open for 0% of the time, Pallas kernels for 0%

commit v1 on v0

v1 whole, which is shorter than its diff:
```python
import functools
import math

import jax
import jax.numpy as jnp
from jax import lax
from jax.experimental import pallas as pl
from jax.experimental.pallas import tpu as pltpu
from jax.sharding import PartitionSpec as P

RPIX = 2048
L = 1024
M_DEV = 256
LANES = 128
FINE = 32
DEPTH = 512
VMEM = 56 * 1024 * 1024
MESH = pl.DeviceIdType.MESH


def cos_sin(phase, half):
    turns = jnp.floor(phase * (0.5 / half))
    rest = phase - turns * (2.0 * half)
    y = (rest - half) * (0.5 * math.pi / half)
    z = y * y
    s = jnp.full_like(z, -1.0 / math.factorial(11))
    for k, sign in ((9, 1), (7, -1), (5, 1), (3, -1), (1, 1)):
        s = s * z + sign / math.factorial(k)
    s = s * y
    c = jnp.full_like(z, 1.0 / math.factorial(12))
    for k, sign in ((10, -1), (8, 1), (6, -1), (4, 1), (2, -1), (0, 1)):
        c = c * z + sign / math.factorial(k)
    return 2.0 * s * s - 1.0, -2.0 * s * c


def whole_numbers(count, step=1, start=0):
    return (start + step * jnp.arange(count, dtype=jnp.int32)).astype(jnp.float32)


def cycle_factors(cycle_len, m_width):
    half = cycle_len.astype(jnp.float32)[:, None, None]
    orders = whole_numbers(m_width)[None, None, :]
    fine = whole_numbers(FINE, 2, 1)[None, :, None] * orders
    coarse = whole_numbers(RPIX // FINE, 2 * FINE)[None, :, None] * orders
    weight = lax.rsqrt(half)
    ac, as_ = cos_sin(fine, half)
    bc, bs = cos_sin(coarse, half)
    return ac * weight, as_ * weight, bc, bs


def theta_table(n_cycle):
    odd = whole_numbers(n_cycle, 2, 1)
    half = jnp.float32(2 * n_cycle)
    cosine, _ = cos_sin(whole_numbers(L)[:, None] * odd[None, :], half)
    weight = jnp.sin(jnp.pi * odd / (2.0 * n_cycle)) * (2.0 / jnp.sqrt(jnp.float32(n_cycle)))
    return (cosine * weight[None, :]).astype(jnp.bfloat16)


def sum_kernel(n_blk, n_grp, part_ref, out_ref, got_blk, got_grp, mid, ssem, rsem, ssem2, rsem2):
    blk, grp = lax.axis_index("blk"), lax.axis_index("grp")
    barrier = pltpu.get_barrier_semaphore()
    for s in range(1, n_blk):
        peer = lax.rem(blk + s, n_blk)
        pl.semaphore_signal(barrier, inc=1, device_id=(peer, grp), device_id_type=MESH)
    for s in range(1, n_grp):
        peer = lax.rem(grp + s, n_grp)
        pl.semaphore_signal(barrier, inc=1, device_id=(blk, peer), device_id_type=MESH)
    pl.semaphore_wait(barrier, n_blk - 1 + n_grp - 1)
    copies = []
    for s in range(1, n_blk):
        copies.append(
            pltpu.make_async_remote_copy(
                src_ref=part_ref,
                dst_ref=got_blk.at[s],
                send_sem=ssem.at[s],
                recv_sem=rsem.at[s],
                device_id=(lax.rem(blk + s, n_blk), grp),
                device_id_type=MESH,
            )
        )
        copies[-1].start()
    got_blk[0] = part_ref[...]
    for copy in copies:
        copy.wait()
    total = jnp.zeros(part_ref.shape, jnp.float32)
    for b in range(n_blk):
        total = total + got_blk[lax.rem(blk - b + n_blk, n_blk)]
    mid[...] = total
    copies = []
    for s in range(1, n_grp):
        copies.append(
            pltpu.make_async_remote_copy(
                src_ref=mid,
                dst_ref=got_grp.at[s],
                send_sem=ssem2.at[s],
                recv_sem=rsem2.at[s],
                device_id=(blk, lax.rem(grp + s, n_grp)),
                device_id_type=MESH,
            )
        )
        copies[-1].start()
    got_grp[0] = total
    for copy in copies:
        copy.wait()
    total = jnp.zeros(part_ref.shape, jnp.float32)
    for g in range(n_grp):
        total = total + got_grp[lax.rem(grp - g + n_grp, n_grp)]
    out_ref[...] = total


def sum_all(part, n_blk, n_grp):
    shape = part.shape
    vmem = pl.BlockSpec(memory_space=pltpu.VMEM)
    return pl.pallas_call(
        functools.partial(sum_kernel, n_blk, n_grp),
        out_shape=jax.ShapeDtypeStruct(shape, jnp.float32),
        in_specs=[vmem],
        out_specs=vmem,
        scratch_shapes=[
            pltpu.VMEM((n_blk,) + shape, jnp.float32),
            pltpu.VMEM((n_grp,) + shape, jnp.float32),
            pltpu.VMEM(shape, jnp.float32),
            pltpu.SemaphoreType.DMA((n_blk,)),
            pltpu.SemaphoreType.DMA((n_blk,)),
            pltpu.SemaphoreType.DMA((n_grp,)),
            pltpu.SemaphoreType.DMA((n_grp,)),
        ],
        compiler_params=pltpu.CompilerParams(
            collective_id=0, has_side_effects=True, vmem_limit_bytes=16 * 1024 * 1024
        ),
        name="sum_all",
    )(part)


def fourier_kernel(n_blk, n_grp, x_ref, ac_ref, as_ref, bc_ref, bs_ref, out_ref, tab, acc):
    k = pl.program_id(1)
    m_width = ac_ref.shape[2]
    chan = out_ref.shape[4]

    def column(t, carry):
        at = pl.multiple_of(t * LANES, LANES)
        ac = ac_ref[0, :, pl.ds(at, LANES)]
        as_ = as_ref[0, :, pl.ds(at, LANES)]
        for i in range(DEPTH // FINE):
            bc = bc_ref[0, pl.ds(i, 1), pl.ds(at, LANES)]
            bs = bs_ref[0, pl.ds(i, 1), pl.ds(at, LANES)]
            rows = pl.ds(i * FINE, FINE)
            tab[rows, pl.ds(at, LANES)] = (ac * bc - as_ * bs).astype(jnp.bfloat16)
            low = pl.multiple_of(m_width + at, LANES)
            tab[rows, pl.ds(low, LANES)] = -(as_ * bc + ac * bs).astype(jnp.bfloat16)
        return carry

    lax.fori_loop(0, m_width // LANES, column, 0)

    @pl.when(k == 0)
    def _():
        acc[...] = jnp.zeros_like(acc)

    for t in range(2 * m_width // 512):
        cols = pl.ds(t * 512, 512)
        acc[:, cols] += jnp.dot(x_ref[...], tab[:, cols], preferred_element_type=jnp.float32)

    @pl.when(k == pl.num_programs(1) - 1)
    def _():
        tiles = M_DEV // LANES
        for g in range(n_grp):
            for mt in range(tiles):
                for p in range(2):
                    at = p * m_width + g * M_DEV + mt * LANES
                    for b in range(n_blk):
                        out_ref[g, b, 0, mt * 2 + p] = acc[
                            b * chan : (b + 1) * chan, at : at + LANES
                        ].astype(jnp.bfloat16)


def fourier_all(cleaned, factors, n_blk, n_grp):
    n_chan = cleaned.shape[0]
    ac, as_, bc, bs = factors
    cycle_dev, _, m_width = ac.shape
    steps = RPIX // DEPTH
    rows = 2 * M_DEV // LANES
    fine = pl.BlockSpec((1, FINE, m_width), lambda c, k: (c, 0, 0))
    coarse = pl.BlockSpec((1, DEPTH // FINE, m_width), lambda c, k: (c, k, 0))
    shape = (n_grp, n_blk, cycle_dev, rows, n_chan // n_blk, LANES)
    return pl.pallas_call(
        functools.partial(fourier_kernel, n_blk, n_grp),
        grid=(cycle_dev, steps),
        out_shape=jax.ShapeDtypeStruct(shape, jnp.bfloat16),
        in_specs=[
            pl.BlockSpec((n_chan, DEPTH), lambda c, k: (0, c * steps + k)),
            fine,
            fine,
            coarse,
            coarse,
        ],
        out_specs=pl.BlockSpec(
            shape[:2] + (1,) + shape[3:], lambda c, k: (0, 0, c, 0, 0, 0)
        ),
        scratch_shapes=[
            pltpu.VMEM((DEPTH, 2 * m_width), jnp.bfloat16),
            pltpu.VMEM((n_chan, 2 * m_width), jnp.float32),
        ],
        compiler_params=pltpu.CompilerParams(vmem_limit_bytes=VMEM),
        name="fourier",
    )(cleaned, ac, as_, bc, bs)


def move_kernel(n_blk, n_grp, src_ref, dst_ref, ssem, rsem, lsem):
    blk, grp = lax.axis_index("blk"), lax.axis_index("grp")
    me = blk * n_grp + grp
    n = n_blk * n_grp
    barrier = pltpu.get_barrier_semaphore()

    def greet(s, carry):
        to = lax.rem(me + s, n)
        pl.semaphore_signal(
            barrier, inc=1, device_id=(to // n_grp, lax.rem(to, n_grp)), device_id_type=MESH
        )
        return carry

    lax.fori_loop(1, n, greet, 0)
    pl.semaphore_wait(barrier, n - 1)

    def copy_of(s):
        to = lax.rem(me + s, n)
        to_blk, to_grp = to // n_grp, lax.rem(to, n_grp)
        return pltpu.make_async_remote_copy(
            src_ref=src_ref.at[to_grp, to_blk],
            dst_ref=dst_ref.at[me],
            send_sem=ssem.at[s],
            recv_sem=rsem.at[s],
            device_id=(to_blk, to_grp),
            device_id_type=MESH,
        )

    def send(s, carry):
        copy_of(s).start()
        return carry

    lax.fori_loop(1, n, send, 0)
    own = pltpu.make_async_copy(src_ref.at[grp, blk], dst_ref.at[me], lsem)
    own.start()
    own.wait()

    def finish(s, carry):
        copy_of(s).wait_send()
        sender = lax.rem(me - s + n, n)
        pltpu.make_async_remote_copy(
            src_ref=src_ref.at[grp, blk],
            dst_ref=dst_ref.at[sender],
            send_sem=ssem.at[s],
            recv_sem=rsem.at[s],
            device_id=(sender // n_grp, lax.rem(sender, n_grp)),
            device_id_type=MESH,
        ).wait_recv()
        return carry

    lax.fori_loop(1, n, finish, 0)


def move_all(fourier, n_blk, n_grp):
    n = n_blk * n_grp
    hbm = pl.BlockSpec(memory_space=pl.ANY)
    return pl.pallas_call(
        functools.partial(move_kernel, n_blk, n_grp),
        out_shape=jax.ShapeDtypeStruct((n,) + fourier.shape[2:], jnp.bfloat16),
        in_specs=[hbm],
        out_specs=hbm,
        scratch_shapes=[
            pltpu.SemaphoreType.DMA((n,)),
            pltpu.SemaphoreType.DMA((n,)),
            pltpu.SemaphoreType.DMA,
        ],
        compiler_params=pltpu.CompilerParams(
            collective_id=1, has_side_effects=True, vmem_limit_bytes=16 * 1024 * 1024
        ),
        name="move_all",
    )(fourier)


def power_kernel(index_ref, x_ref, g_ref, mw_ref, out_ref):
    c = pl.program_id(0)
    own = index_ref[c]
    total = jnp.zeros((1, LANES), jnp.float32)
    tiles = M_DEV // LANES
    for mt in range(tiles):
        x = jnp.concatenate([x_ref[0, mt * 2], x_ref[0, mt * 2 + 1]], axis=1)
        z = jnp.dot(g_ref[own, 0], x, preferred_element_type=jnp.float32)
        z = z + jnp.dot(g_ref[own, 1], x, preferred_element_type=jnp.float32)
        sums = jnp.sum(z * x.astype(jnp.float32), axis=0, keepdims=True)
        mw = mw_ref[pl.ds(mt, 1), :]
        total = total + (sums[:, :LANES] + sums[:, LANES:]) * (mw * mw)
    out_ref[0] = jnp.broadcast_to(total, (8, LANES))


def power_of(index, x, gram, mweight):
    chan_dev, rows, n_cycle, _ = x.shape
    out = pl.pallas_call(
        power_kernel,
        grid_spec=pltpu.PrefetchScalarGridSpec(
            num_scalar_prefetch=1,
            grid=(chan_dev,),
            in_specs=[
                pl.BlockSpec((1, rows, n_cycle, LANES), lambda c, i: (c, 0, 0, 0)),
                pl.BlockSpec(gram.shape, lambda c, i: (0, 0, 0, 0)),
                pl.BlockSpec(mweight.shape, lambda c, i: (0, 0)),
            ],
            out_specs=pl.BlockSpec((1, 8, LANES), lambda c, i: (c, 0, 0)),
        ),
        out_shape=jax.ShapeDtypeStruct((chan_dev, 8, LANES), jnp.float32),
        compiler_params=pltpu.CompilerParams(vmem_limit_bytes=VMEM),
        name="power",
    )(index, x, gram, mweight)
    return jnp.sum(out[:, 0, :], axis=1)


def result_kernel(x_ref, theta_ref, w_ref, mw_ref, out_ref):
    step = pl.program_id(0)
    tiles = M_DEV // LANES
    rows = 2 * tiles
    pair = out_ref.shape[1] // rows
    lanes = w_ref.shape[1]
    shift = lax.rem(lanes - pair * step, lanes)
    part = 256
    for at in range(0, L, part):
        w = pltpu.roll(w_ref[at : at + part, :], shift, 1)
        for c in range(pair):
            own = jnp.broadcast_to(w[:, c : c + 1], (part, LANES))
            for mt in range(tiles):
                scale = own * mw_ref[mt : mt + 1, :]
                x = jnp.concatenate([x_ref[c, mt * 2], x_ref[c, mt * 2 + 1]], axis=1)
                h = jnp.dot(theta_ref[at : at + part, :], x, preferred_element_type=jnp.float32)
                row = c * rows + mt * 2
                out_ref[at : at + part, row, :] = h[:, :LANES] * scale
                out_ref[at : at + part, row + 1, :] = h[:, LANES:] * scale


def result_of(x, theta_tab, w, mweight):
    chan_dev, rows, n_cycle, _ = x.shape
    pair = 8 // rows
    full = lambda a: pl.BlockSpec(a.shape, lambda c: (0,) * a.ndim)
    return pl.pallas_call(
        result_kernel,
        grid=(chan_dev // pair,),
        out_shape=jax.ShapeDtypeStruct((L, chan_dev * rows, LANES), jnp.float32),
        in_specs=[
            pl.BlockSpec((pair, rows, n_cycle, LANES), lambda c: (c, 0, 0, 0)),
            full(theta_tab),
            full(w),
            full(mweight),
        ],
        out_specs=pl.BlockSpec((L, pair * rows, LANES), lambda c: (0, c, 0)),
        compiler_params=pltpu.CompilerParams(vmem_limit_bytes=VMEM),
        name="result",
    )(x, theta_tab, w, mweight)


def body(sky_map, fg_templates, cycle_len, beam_profile, beam_index):
    n_blk = lax.axis_size("blk")
    n_grp = lax.axis_size("grp")
    cycle_dev = cycle_len.shape[0]
    n_chan = sky_map.shape[0]
    n_mode = fg_templates.shape[1]
    chan_dev = n_chan // n_blk
    m_width = M_DEV * n_grp
    n_cycle = cycle_dev * n_blk * n_grp
    slots = jnp.arange(RPIX, dtype=jnp.int32)
    valid = (slots[None, :] < cycle_len[:, None]).reshape(-1)
    masked = jnp.where(valid[None, :], sky_map, jnp.zeros((), jnp.bfloat16))
    mode_amps = jnp.dot(fg_templates.T, masked, preferred_element_type=jnp.float32).astype(
        jnp.bfloat16
    )
    gram_part = jnp.dot(mode_amps, mode_amps.T, preferred_element_type=jnp.float32)
    cross_part = lax.dot_general(
        mode_amps, masked, (((1,), (1,)), ((), ())), preferred_element_type=jnp.float32
    )
    fill = jnp.zeros((n_mode, LANES - n_mode), jnp.float32)
    sums = sum_all(jnp.concatenate([cross_part, gram_part, fill], axis=1), n_blk, n_grp)
    lower = jnp.linalg.cholesky(sums[:, n_chan : n_chan + n_mode])
    basis = jax.scipy.linalg.solve_triangular(lower, mode_amps.astype(jnp.float32), lower=True)
    projected = jax.scipy.linalg.solve_triangular(lower, sums[:, :n_chan], lower=True)
    correction = jnp.dot(projected.T, basis, precision=lax.Precision.HIGHEST)
    cleaned = (masked.astype(jnp.float32) - correction).astype(jnp.bfloat16)
    cleaned = jnp.where(valid[None, :], cleaned, jnp.zeros((), jnp.bfloat16))
    fourier = fourier_all(cleaned, cycle_factors(cycle_len, m_width), n_blk, n_grp)
    moved = move_all(fourier, n_blk, n_grp)
    rows = fourier.shape[3]
    x = moved.reshape(n_cycle, rows, chan_dev, LANES).transpose(2, 1, 0, 3)

    theta_tab = theta_table(n_cycle)
    theta_wide = theta_tab.astype(jnp.float32)
    squared = (beam_profile * beam_profile)[:, :, None] * theta_wide[None]
    gram = jnp.einsum("plr,ls->prs", squared, theta_wide, precision=lax.Precision.HIGHEST)
    high = gram.astype(jnp.bfloat16)
    low = (gram - high.astype(jnp.float32)).astype(jnp.bfloat16)
    gram = jnp.stack([high, low], 1)
    orders = lax.axis_index("grp") * M_DEV + jnp.arange(M_DEV, dtype=jnp.int32)
    mweight = (0.25 + orders.astype(jnp.float32) / m_width).reshape(M_DEV // LANES, LANES)
    power = lax.psum(power_of(beam_index, x, gram, mweight), "grp")
    onehot = (
        beam_index[:, None] == jnp.arange(beam_profile.shape[0], dtype=jnp.int32)[None, :]
    ).astype(jnp.float32)
    profiles = jnp.dot(onehot, beam_profile, precision=lax.Precision.HIGHEST)
    scaled = profiles * lax.rsqrt(power / (2.0 * L * m_width) + 1e-06)[:, None]
    w = jnp.pad(scaled.T, ((0, 0), (0, LANES - chan_dev)))
    out = result_of(x, theta_tab, w, mweight)
    out = out.reshape(L, chan_dev, M_DEV // LANES, 2, LANES).transpose(0, 1, 3, 2, 4)
    return out.reshape(L, chan_dev, 2, M_DEV)


def solution(mesh):
    return jax.shard_map(
        body,
        mesh=mesh,
        in_specs=(P(None, ("blk", "grp")), P(), P(("blk", "grp")), P(), P("blk")),
        out_specs=P(None, "blk", None, "grp"),
        check_vma=False,
    )
```

time: 1090 us -> 261 us (0.24)
  other arithmetic: 511 us -> 15.4 us
  local copies, waits for them, and re-layouts: 250 us -> 8.56 us
  Pallas kernels: 0 us -> 207 us
  blocking collectives: 145 us -> 11.9 us
  waiting for transfers between devices: 92.5 us -> 0 us
  matrix products: 75.8 us -> 17.1 us
    cos x1 -> x0, other arithmetic: 451 us -> none  [cycle_table(): jnp.cos(angle)]
    pallas_call x0 -> x5, Pallas kernels: none -> 207 us  [the longest x1 94 us: move_all(): pl.pallas_call(functools.partial(move_kernel, n_blk, n_grp), out_shape=ja...]
    mul x1 -> x0, local copies, waits for them, and re-layouts: 108 us -> none  [body(): weighted * lax.rsqrt(power / (2.0 * L * m_width) + 1e-06)[None, :, None,...]
    all_to_all x1 -> x0, waiting for transfers between devices: 92.5 us -> none  [body(): lax.all_to_all(lax.all_to_all(fourier, 'blk', split_axis=1, concat_axis=0...]
    all_to_all x5 -> x0, local copies, waits for them, and re-layouts: 89.2 us -> none  [the longest x2 49.4 us: body(): lax.all_to_all(lax.all_to_all(fourier, 'blk', split_axis=1, concat_axis=0...]
    psum x3 -> x1, blocking collectives: 92.1 us -> 11.9 us  [body(): power = lax.psum(power_of(beam_index, x, gram, mweight), 'grp')]
    dot_general x5 -> x1, matrix products: 59.6 us -> 2.54 us  [body(): jnp.einsum('plr,ls->prs', squared, theta_wide, precision=lax.Precision.HI...]
    all_to_all x1 -> x0, blocking collectives: 53.2 us -> none  [body(): lax.all_to_all(fourier, 'blk', split_axis=1, concat_axis=0, tiled=True)]
  transfers between devices with their start and end apart: 1 -> 0, of which waited for: 1 -> 0; matrix products, arithmetic and copies ran while one was open for 0% -> 0% of each run, Pallas kernels for 0% -> 0%
where the time goes in v1:
time: 261 us; the launch traced here: 260 us
  Pallas kernels  207 us (79%)
  matrix products  17.1 us (7%)
  other arithmetic  15.4 us (6%)
  blocking collectives  11.9 us (5%)
  local copies, waits for them, and re-layouts  8.56 us (3%)
    pallas_call x1, Pallas kernels, move_all(): pl.pallas_call(functools.partial(move_kernel, n_blk, n_grp), out_shape=ja...  94 us
    pallas_call x1, Pallas kernels, result_of(): pl.pallas_call(result_kernel, grid=(chan_dev // pair,), out_shape=jax.Sha...  47.9 us
    pallas_call x1, Pallas kernels, fourier_all(): pl.pallas_call(functools.partial(fourier_kernel, n_blk, n_grp), grid=(cyc...  31.3 us
    pallas_call x1, Pallas kernels, power_of(): pl.pallas_call(power_kernel, grid_spec=pltpu.PrefetchScalarGridSpec(num_s...  20.8 us
    pallas_call x1, Pallas kernels, sum_all(): pl.pallas_call(functools.partial(sum_kernel, n_blk, n_grp), out_shape=jax...  13.2 us
    psum x1, blocking collectives, body(): power = lax.psum(power_of(beam_index, x, gram, mweight), 'grp')  11.9 us
    dot_general x1, matrix products, body(): correction = jnp.dot(projected.T, basis, precision=lax.Precision.HIGHEST)  9.05 us

profile of v1, /device:TPU:0, one launch (start us, length us, event | category | flops | bytes accessed | tf_op | source)
XLA Modules:
  0.0 260.3 jit_solution(17215139233160440036)
XLA Ops:
  0.0 0.8 convert_element_type.105
  0.8 0.6 multiply_add_fusion.mw_ref
  1.6 0.7 broadcast_divide_fusion.1
  2.2 0.7 fusion.30
  3.0 0.8 mul.578
  4.0 2.9 %convolution_convert_fusion = bf16[8192,16]{0,1:T(8,128)(2,1)S(1)} fusion(bf16[256,16]{0,1:T(8,128)(2,1)S(1)} %copy-done, bf16[256,8192]{1,0:T(8,128)(2,1)} %param.5, pred[8192]{0:T(1024)(128)(4,1)S(1)} %bitcast.45), kind=kOutput, calls=%fused_computation.3 | convolution fusion | flops 69337088 | bytes 4472832 | tf_op jit(solution)/shard_map/dot_general | solution.py:370
  6.8 0.2 fusion.59
  7.1 1.2 fusion.4
  8.3 13.2 %sum_all.1 = f32[16,384]{1,0:T(8,128)S(1)} custom-call(f32[16,384]{1,0:T(8,128)S(1)} %maximum_maximum_fusion.part_ref), custom_call_target="tpu_custom_call" | custom-call | tf_op jit(solution)/shard_map/sum_all/pallas_call | solution.py:114
  21.6 1.5 cholesky.16
  23.1 0.6 compare_reduce_fusion
  23.8 0.6 fusion.35
  24.4 1.2 custom-call.10
  25.6 0.2 fusion.31
  25.8 0.4 fusion.36
  26.3 1.2 fusion.34
  27.5 0.2 copy.16
  27.7 2.5 convert_bitcast_fusion
  30.2 0.9 pad_maximum_fusion.g_ref
  31.1 1.7 multiply_multiply_fusion.7
  32.7 2.6 add_multiply_fusion
  35.3 9.0 %fusion.1.x_ref = bf16[256,8192]{1,0:T(8,128)(2,1)} fusion(f32[16,256]{1,0:T(8,128)S(1)} %fusion.31, f32[16,8192]{1,0:T(8,128)S(1)} %fusion.36, pred[8192]{0:T(1024)(128)(4,1)S(1)} %bitcast.47, bf16[256,8192]{1,0:T(8,128)(2,1)S(1)} %copy-done.5), kind=kOutput, calls=%fused_computation.2 | convolution fusion | flops 413138944 | bytes 8937472 | tf_op jit(solution)/shard_map/dot_general | solution.py:382
  44.4 31.3 %fourier.1.src_ref = bf16[4,8,4,4,32,128]{5,4,3,2,1,0:T(8,128)(2,1)} custom-call(bf16[256,8192]{1,0:T(8,128)(2,1)} %fusion.1.x_ref, f32[4,32,1024]{2,1,0:T(8,128)} %get-tuple-element.10.ac_ref, f32[4,32,1024]{2,1,0:T(8,128)} %get-tuple-element.9.as_ref, f32[4,64,1024]{2,1,0:T(8,128)} %get-tuple-element.8.bc_ref, f32[4,64,1024]{2,1,0:T(8,128)} %get-tuple-element.7.bs_ref), custom_call_target="tpu_custom_call" | custom-call | tf_op jit(solution)/shard_map/fourier/pallas_call | solution.py:185
  75.7 2.2 copy-done.1
  77.9 94.0 %move_all.1 = bf16[32,4,4,32,128]{4,3,2,1,0:T(8,128)(2,1)S(1)} custom-call(bf16[4,8,4,4,32,128]{5,4,3,2,1,0:T(8,128)(2,1)S(1)} %copy-done.1), custom_call_target="tpu_custom_call" | custom-call | tf_op jit(solution)/shard_map/move_all/pallas_call | solution.py:264
  171.9 5.2 %copy.15 = bf16[32,4,4,32,128]{4,1,0,2,3:T(4,128)(2,1)} copy(bf16[32,4,4,32,128]{4,3,2,1,0:T(8,128)(2,1)S(1)} %move_all.1) | data formatting | bytes 8388608 | tf_op jit(solution)/shard_map/move_all/pallas_call | solution.py:264
  177.1 20.8 %power.1 = f32[32,8,128]{2,1,0:T(8,128)} custom-call(s32[32]{0:T(128)} %index_ref.1, bf16[32,4,128,128]{3,2,1,0:T(8,128)(2,1)} %bitcast.43, bf16[8,2,128,128]{3,2,1,0:T(8,128)(2,1)} %pad_maximum_fusion.g_ref, f32[2,128]{1,0:T(2,128)} %multiply_add_fusion.mw_ref), custom_call_target="tpu_custom_call" | custom-call | tf_op jit(solution)/shard_map/power/pallas_call | solution.py:298
  197.8 1.2 slice_reduce_fusion
  199.0 11.9 %psum.7 = f32[32]{0:T(128)S(1)} all-reduce(f32[32]{0:T(128)S(1)} %slice_reduce_fusion), channel_id=1, replica_groups=mesh['blk'=8,'grp'=4] {'grp'}, use_global_device_ids=true, to_apply=%region_3.4 | all-reduce | flops 32 | bytes 256 | tf_op jit(solution)/shard_map/psum | solution.py:399
  211.0 0.6 fusion.9
  211.6 0.8 pad.4.w_ref
  212.4 47.9 %result.1 = f32[1024,128,128]{2,1,0:T(8,128)} custom-call(bf16[32,4,128,128]{3,2,1,0:T(8,128)(2,1)} %bitcast.44, bf16[1024,128]{1,0:T(8,128)(2,1)} %get-tuple-element.12.theta_ref, f32[1024,128]{1,0:T(8,128)} %pad.4.w_ref, f32[2,128]{1,0:T(2,128)} %multiply_add_fusion.mw_ref), custom_call_target="tpu_custom_call" | custom-call | tf_op jit(solution)/shard_map/result/pallas_call | solution.py:342
  (27 shorter events, 0.5 us)
Async XLA Ops:
  0.0 4.0 %copy-start = (bf16[256,16]{0,1:T(8,128)(2,1)S(1)}, bf16[256,16]{0,1:T(8,128)(2,1)}, u32[]{:S(2)}) copy-start(bf16[256,16]{0,1:T(8,128)(2,1)} %param.6) | copy-start | bytes 24580
  0.0 7.1 %copy-start.4 = (bf16[256,8192]{1,0:T(8,128)(2,1)S(1)}, bf16[256,8192]{1,0:T(8,128)(2,1)}, u32[]{:S(2)}) copy-start(bf16[256,8192]{1,0:T(8,128)(2,1)} %param.5) | copy-start | bytes 12582916
  27.7 7.7 %copy-start.5 = (bf16[256,8192]{1,0:T(8,128)(2,1)S(1)}, bf16[256,8192]{1,0:T(8,128)(2,1)}, u32[]{:S(2)}) copy-start(bf16[256,8192]{1,0:T(8,128)(2,1)} %param.5) | copy-start | bytes 12582916
  75.7 2.2 copy-start.1
  177.0 33.9 %copy-start.2 = (f32[8,1024]{1,0:T(8,128)S(1)}, f32[8,1024]{1,0:T(8,128)}, u32[]{:S(2)}) copy-start(f32[8,1024]{1,0:T(8,128)} %param.8) | copy-start | bytes 98308
  177.0 33.9 %copy-start.3 = (s32[32]{0:T(128)S(1)}, s32[32]{0:T(128)}, u32[]{:S(2)}) copy-start(s32[32]{0:T(128)} %index_ref.1) | copy-start | bytes 388
